TPU v7x, 128 devices: a whole 4x4x4 slice. The times are simulated.
128 devices in a mesh: seg: 8 (over y, core), freq: 4 (over z), blk: 4 (over x).
Axes of the slice: x: 4, y: 4, z: 4, core: 2. Of those that a mesh axis runs over, the one named last changes fastest.
Arguments:
- samples: bfloat16 [64, 4096, 2048], P(('seg', 'freq'), 'blk'), may hold values from -100 to 100, as said below
- valid_counts: int32 [32], P('blk'), may hold values from 16 to 128, as said below
- channel_mask: int32 [4096], P('blk'), may hold values 0 or 1
- block_pairs: int32 [16, 2], P('blk'), may hold values from 0 to 31, as said below
Outputs:
- stacked: bfloat16 [16, 1024, 2, 128, 128], P('blk', ('seg', 'freq'))
Inputs may be any that keep to these rules, and one draw needn't show every extreme that they name: A segment's samples are a scale of its own for each segment and channel times values of order one. `valid_counts`: some block has all 128 channels valid. `block_pairs`: the rows of one index d of blk name a first block in d * 8 to (d + 1) * 8 - 1 and a partner that is 0 to 4 blocks after it; on index 0 one row reaches 4.
All inputs are finite; a program needn't handle non-finite values. No bound on the sum of `channel_mask` on one device may be relied on, other than what follows from the above.
Results may differ from a plain program's by a relative error of at most 0.0064.
Values may be sent and summed in bfloat16 or wider, within the bound.
No kernel may reach another device: no remote copies, remote signals or barrier semaphores. Data moves between devices by JAX's collectives and lax.ppermute only.
A program may use at most 128 MiB of HBM per device.

v0:
```python
import math

import jax
import jax.numpy as jnp
import numpy as np
from jax import lax
from jax.experimental import pallas as pl
from jax.experimental.pallas import tpu as pltpu
from jax.sharding import PartitionSpec as P

WIDTH = 128
HB = 4
SIZES = ((128, 320), (192, 320), (256, 448), (320, 448), (512, 512))
VMEM = 60 * 1024 * 1024
NEXT = 1 << 16


def transform_table(bins, samples_len):
    times = np.arange(samples_len, dtype=np.int64)
    order = np.arange(bins, dtype=np.int64)
    phase = (order[:, None] * times[None, :]) % samples_len
    angle = phase * (2.0 * math.pi / samples_len)
    taper = 0.5 - 0.5 * np.cos(times * (2.0 * math.pi / samples_len))
    table = np.stack([taper * np.cos(angle), -taper * np.sin(angle)], 1)
    return table.reshape(2 * bins, samples_len).astype(np.float32).astype(jnp.bfloat16)


def regroup_matrix():
    out = np.zeros((256, 256), np.float32)
    for src in range(16):
        for row in range(16):
            out[row * 16 + src, src * 16 + row] = 1.0
    return out.astype(jnp.bfloat16)


def whole_tiles(count):
    return (count + WIDTH - 1) // WIDTH * WIDTH


def plan_kernel(block_count, me_ref, own_ref, n1_ref, n2_ref, n3_ref, place_ref, where_ref, info_ref, branch_ref):
    refs = (own_ref, n1_ref, n2_ref, n3_ref)
    planes = len(refs)
    me = me_ref[0, 0]
    pairs = where_ref.shape[0] // 2
    firsts = [ref[block_count : block_count + 1, :pairs] for ref in refs]
    partners = [ref[block_count + 1 : block_count + 2, :pairs] for ref in refs]
    flat = lambda x: x.astype(jnp.float32).astype(jnp.bfloat16)
    upto = flat(
        (lax.broadcasted_iota(jnp.int32, (WIDTH, WIDTH), 0) <= lax.broadcasted_iota(jnp.int32, (WIDTH, WIDTH), 1)).astype(jnp.int32)
    )
    row_of = lax.broadcasted_iota(jnp.int32, (block_count, 1), 0)

    def flags(j):
        ids = row_of + lax.rem(me + j, planes) * block_count
        named = jnp.zeros((block_count, 1), jnp.int32)
        rim = jnp.zeros((block_count, 1), jnp.int32)
        for first, partner in zip(firsts, partners):
            hit = partner == ids
            crosses = (first // block_count) != (partner // block_count)
            named = named + jnp.sum((hit | (first == ids)).astype(jnp.int32), axis=1, keepdims=True)
            rim = rim + jnp.sum((hit & crosses).astype(jnp.int32), axis=1, keepdims=True)
        return ids, named > 0, rim > 0

    def ranks(chosen):
        inside = jnp.dot(flat(chosen), upto, preferred_element_type=jnp.float32)
        sums = inside[:, WIDTH - 1 :]
        before = jnp.zeros((block_count, 1), jnp.float32)
        for b in range(block_count - 1):
            before = before + jnp.where(row_of > b, sums[b : b + 1], 0.0)
        return (inside + before).astype(jnp.int32) - 1, jnp.sum(sums, axis=0, keepdims=True).astype(jnp.int32)

    rim_most = jnp.zeros((1, 1), jnp.int32)
    all_list, low_list = [], []
    for j in range(planes):
        ids, named, rim = flags(j)
        valid = refs[j][:block_count]
        counts = jnp.sum(valid, axis=1, keepdims=True)
        total = lambda m: jnp.sum(jnp.where(m, counts, 0), axis=0, keepdims=True)
        rim_most = jnp.maximum(rim_most, total(rim))
        all_list.append(total(named))
        low_list.append(total(named & (row_of < HB)))
        if j == 0:
            own_ids = ids
            rim_mask = jnp.where(rim, valid, 0)
            rest_mask = jnp.where(named & jnp.logical_not(rim), valid, 0)
            rim_rank, rim_count = ranks(rim_mask)
            rest_rank, _ = ranks(rest_mask)
            place = jnp.where(rim_mask > 0, rim_rank, jnp.where(rest_mask > 0, rest_rank + rim_count, -1))
        if j == 1:
            next_ids = ids
            next_mask = jnp.where(rim, valid, 0)
            next_rank, _ = ranks(next_mask)
            next_place = jnp.where(next_mask > 0, next_rank + NEXT, -1)
    branch = jnp.zeros((1, 1), jnp.int32) + (len(SIZES) - 1)
    for n in reversed(range(len(SIZES) - 1)):
        r, l = SIZES[n]
        fits = rim_most <= r
        for everything, low in zip(all_list, low_list):
            fits = fits & (everything - jnp.minimum(low, r) <= l)
        branch = jnp.where(fits, n, branch)
    size = jnp.zeros((1, 1), jnp.int32)
    for n, (r, _) in enumerate(SIZES):
        size = jnp.where(branch == n, r, size)
    behind = jnp.where(row_of >= HB, jnp.maximum(size - low_list[0], 0), 0)
    place = jnp.where(place >= 0, place + behind + whole_tiles(size) - size, -1)
    place_ref[...] = place

    def look(block):
        here = jnp.max(jnp.where(own_ids == block, place, -1), axis=0, keepdims=True)
        beyond = jnp.max(jnp.where(next_ids == block, next_place, -1), axis=0, keepdims=True)
        return jnp.maximum(here, beyond)

    found = [look(firsts[0][:, p : p + 1]) for p in range(pairs)] + [look(partners[0][:, p : p + 1]) for p in range(pairs)]
    found = jnp.concatenate(found, 0)
    where_ref[...] = found
    starts = jnp.min(jnp.where(found >= 0, found, 2 * NEXT), axis=1, keepdims=True)
    starts = jnp.where(starts == 2 * NEXT, 0, starts)
    lanes = lax.broadcasted_iota(jnp.int32, info_ref.shape, 1)
    info_ref[...] = jnp.where(lanes == 0, starts, 0)
    branch_ref[0, 0] = jnp.max(branch)


def plan(me, own, others, block_count, pairs):
    vmem = pl.BlockSpec(memory_space=pltpu.VMEM)
    return pl.pallas_call(
        lambda *refs: plan_kernel(block_count, *refs),
        in_specs=[pl.BlockSpec(memory_space=pltpu.SMEM)] + [vmem] * 4,
        out_specs=[vmem] * 3 + [pl.BlockSpec(memory_space=pltpu.SMEM)],
        out_shape=[
            jax.ShapeDtypeStruct((block_count, WIDTH), jnp.int32),
            jax.ShapeDtypeStruct((2 * pairs, WIDTH), jnp.int32),
            jax.ShapeDtypeStruct((2 * pairs, WIDTH), jnp.int32),
            jax.ShapeDtypeStruct((1, 1), jnp.int32),
        ],
    )(me, own, *others)


def spectra_kernel(base, count, tile, across, place_ref, samples_ref, table_ref, out_ref, held, table, picked, spectra, power, ready, held_sem, table_sem, out_sem):
    segs, channels, samples_len = held.shape
    lanes = picked.shape[0]
    pieces = table_sem.shape[0]
    rows = table.shape[0] // pieces

    get = [pltpu.make_async_copy(samples_ref.at[s, :channels, :], held.at[s], held_sem.at[s]) for s in range(segs)]
    for copy in get:
        copy.start()

    def table_copy(n):
        here = pl.ds(pl.multiple_of(n * rows, rows), rows)
        return pltpu.make_async_copy(table_ref.at[here, :], table.at[here, :], table_sem.at[n])

    @pl.loop(0, pieces)
    def _(n):
        table_copy(n).start()

    target = lax.broadcasted_iota(jnp.int32, (count, channels), 0) + base
    chosen = (place_ref[:, :channels] == target).astype(jnp.bfloat16)
    for s in range(segs):
        get[s].wait()

        @pl.loop(0, samples_len // tile)
        def _(n):
            cols = pl.ds(pl.multiple_of(n * tile, tile), tile)
            found = jnp.dot(chosen, held[s, :, cols], preferred_element_type=jnp.float32)
            picked[s * count : (s + 1) * count, cols] = found.astype(jnp.bfloat16)

    power[...] = jnp.zeros(power.shape, jnp.float32)

    @pl.loop(0, pieces)
    def _(n):
        here = pl.ds(pl.multiple_of(n * rows, rows), rows)
        table_copy(n).wait()

        @pl.loop(0, lanes // across)
        def _(m):
            cols = pl.ds(pl.multiple_of(m * across, across), across)
            block = lax.dot_general(
                table[here, :], picked[cols, :], (((1,), (1,)), ((), ())), preferred_element_type=jnp.float32
            )
            spectra[here, cols] = block
            power[:, cols] = power[:, cols] + jnp.sum((block * block).reshape(rows // 8, 8, across), axis=0)

    scale = lax.rsqrt(jnp.sum(power[...], axis=0, keepdims=True) / (table.shape[0] // 2) + 1e-06)
    peers, each, _ = ready.shape
    quarter = peers // out_sem.shape[0]

    def send(n):
        here = pl.ds(pl.multiple_of(n * quarter, quarter), quarter)
        return pltpu.make_async_copy(ready.at[here], out_ref.at[here], out_sem.at[n])

    @pl.loop(0, out_sem.shape[0])
    def _(n):
        @pl.loop(0, quarter)
        def _(j):
            peer = n * quarter + j
            here = pl.ds(pl.multiple_of(peer * each, each), each)
            ready[peer] = (spectra[here, : segs * count] * scale[:, : segs * count]).astype(jnp.bfloat16)

        send(n).start()

    @pl.loop(0, out_sem.shape[0])
    def _(n):
        send(n).wait()


def spectra_chunk(samples, table, place, channels, base, count, peers, urgent):
    segs, _, samples_len = samples.shape
    rows_total = table.shape[0]
    lanes = segs * count
    pieces, tile, across = (4, 1024, lanes) if urgent else (4, 256, 256)
    wide = (lanes + across - 1) // across * across
    body = lambda *refs: spectra_kernel(base, count, tile, across, *refs)
    hbm = pl.BlockSpec(memory_space=pl.ANY)
    vmem = pl.BlockSpec(memory_space=pltpu.VMEM)
    return pl.pallas_call(
        body,
        in_specs=[vmem, hbm, hbm],
        out_specs=hbm,
        out_shape=jax.ShapeDtypeStruct((peers, rows_total // peers, lanes), jnp.bfloat16),
        scratch_shapes=[
            pltpu.VMEM((segs, channels, samples_len), jnp.bfloat16),
            pltpu.VMEM((rows_total, samples_len), jnp.bfloat16),
            pltpu.VMEM((wide, samples_len), jnp.bfloat16),
            pltpu.VMEM((rows_total, wide), jnp.float32),
            pltpu.VMEM((8, wide), jnp.float32),
            pltpu.VMEM((peers, rows_total // peers, lanes), jnp.bfloat16),
            pltpu.SemaphoreType.DMA((segs,)),
            pltpu.SemaphoreType.DMA((pieces,)),
            pltpu.SemaphoreType.DMA((4,)),
        ],
        compiler_params=pltpu.CompilerParams(vmem_limit_bytes=VMEM + 7 * 512 * 1024),
        cost_estimate=pl.CostEstimate(
            flops=2 * segs * count * samples_len * (rows_total + channels),
            bytes_accessed=2 * (segs * channels * samples_len + rows_total * samples_len),
            transcendentals=0,
        ),
    )(place, samples, table)


def after(value, other):
    def nothing(value_ref, other_ref, out_ref):
        del value_ref, other_ref, out_ref

    anywhere = pl.BlockSpec(memory_space=pl.ANY)
    return pl.pallas_call(
        nothing,
        in_specs=[anywhere, anywhere],
        out_specs=anywhere,
        out_shape=jax.ShapeDtypeStruct(value.shape, value.dtype),
        input_output_aliases={0: 0},
        compiler_params=pltpu.CompilerParams(vmem_limit_bytes=VMEM + 7 * 512 * 1024),
        cost_estimate=pl.CostEstimate(flops=10**11, bytes_accessed=2**30, transcendentals=0),
    )(value, other)


def stack_kernel(counts, scale, info_ref, where_ref, regroup_ref, xr_ref, xl_ref, zr_ref, out_ref, pick_l, pick_r, held):
    r_count, l_count = counts
    own = whole_tiles(r_count) + whole_tiles(l_count)
    pairs, bins, _, width, _ = out_ref.shape
    window = 2 * width
    behind = own + whole_tiles(r_count) - r_count - NEXT

    def start(n):
        first = info_ref[n, 0]
        first = jnp.where(first >= NEXT, first + behind, first)
        return pl.multiple_of((first // width) * width, width)

    @pl.when(pl.program_id(0) == 0)
    def _():
        held[:, held.shape[1] - width :] = jnp.zeros((held.shape[0], width), held.dtype)
        where = where_ref[...]
        where = jnp.where(where >= NEXT, where + behind, where)
        eye = lax.broadcasted_iota(jnp.int32, (width, width), 0) == lax.broadcasted_iota(jnp.int32, (width, width), 1)
        for p in range(pairs):
            pick_l[p] = (where[p : p + 1] == lax.broadcasted_iota(jnp.int32, (window, width), 0) + start(p)).astype(jnp.bfloat16) * jnp.bfloat16(scale)
            row = where[pairs + p : pairs + p + 1]
            pick_r[p] = (row == lax.broadcasted_iota(jnp.int32, (window, width), 0) + start(pairs + p)).astype(jnp.bfloat16)

    chunks = ((xr_ref, r_count, 0, True), (xl_ref, l_count, whole_tiles(r_count), False), (zr_ref, r_count, own, True))
    for ref, count, at, to_end in chunks:
        full = whole_tiles(count)
        for h in range(2):
            rows = ref[h * 16 : (h + 1) * 16].reshape(256, 2 * count)
            rows = jnp.dot(regroup_ref[...], rows, preferred_element_type=jnp.float32)
            by_seg = [rows[:, :full], rows[:, 2 * count - full :]]
            if full != count:
                turn = 0 if to_end else 1
                by_seg[turn] = pltpu.roll(by_seg[turn], WIDTH // 2 if to_end else full - WIDTH // 2, 1)
            for s in range(2):
                part = by_seg[s].astype(jnp.bfloat16)
                for k in range(bins):
                    to = k * 128 + (s * 2 + h) * 32
                    held[to : to + 32, at : at + full] = part[k * 32 : (k + 1) * 32]

    def one_pair(p):
        from_l = held[:, pl.ds(start(p), window)]
        left = jnp.dot(from_l, pick_l[p], preferred_element_type=jnp.float32)
        left = left.astype(jnp.bfloat16)
        from_r = held[:, pl.ds(start(pairs + p), window)]
        right = jnp.dot(from_r, pick_r[p], preferred_element_type=jnp.float32).astype(jnp.bfloat16)
        for k in range(bins):
            b = right[k * 128 : (k + 1) * 128]
            turned = []
            for g in range(4):
                turned.append(-b[g * 32 + 16 : g * 32 + 32])
                turned.append(b[g * 32 : g * 32 + 16])
            both = jnp.concatenate([b, jnp.concatenate(turned, 0)], 1)
            a = left[k * 128 : (k + 1) * 128]
            res = (lax.dot_general(a, both, (((0,), (0,)), ((), ())), preferred_element_type=jnp.float32)).astype(jnp.bfloat16)
            out_ref[p, k, 0] = res[:, :width]
            out_ref[p, k, 1] = res[:, width:]

    pl.loop(0, pairs, unroll=4 if r_count < 256 else 1)(one_pair)


def stacked_products(xr, xl, zr, info, where, regroup, pairs, scale):
    peers, rows, r_two = xr.shape
    l_two = xl.shape[2]
    r_count, l_count = r_two // 2, l_two // 2
    bins = rows // 2
    group = 8
    body = lambda *refs: stack_kernel((r_count, l_count), scale, *refs)
    whole = lambda shape: pl.BlockSpec(shape, lambda g: (0,) * len(shape))
    part = lambda lanes: pl.BlockSpec((peers, 2 * group, lanes), lambda g: (0, g, 0))
    return pl.pallas_call(
        body,
        grid=(bins // group,),
        in_specs=[
            pl.BlockSpec(memory_space=pltpu.SMEM), whole(where.shape), whole((256, 256)),
            part(r_two), part(l_two), part(r_two),
        ],
        out_specs=pl.BlockSpec((pairs, group, 2, WIDTH, WIDTH), lambda g: (0, g, 0, 0, 0)),
        out_shape=jax.ShapeDtypeStruct((pairs, bins, 2, WIDTH, WIDTH), jnp.bfloat16),
        scratch_shapes=[
            pltpu.VMEM((pairs, 2 * WIDTH, WIDTH), jnp.bfloat16),
            pltpu.VMEM((pairs, 2 * WIDTH, WIDTH), jnp.bfloat16),
            pltpu.VMEM((group * 128, 2 * whole_tiles(r_count) + whole_tiles(l_count) + WIDTH), jnp.bfloat16),
        ],
        compiler_params=pltpu.CompilerParams(vmem_limit_bytes=VMEM),
        cost_estimate=pl.CostEstimate(
            flops=2 * peers * rows * 2 * WIDTH * (4 * pairs * WIDTH + 2 * r_two + l_two),
            bytes_accessed=2 * (peers * rows * (2 * r_two + l_two) + pairs * bins * 2 * WIDTH * WIDTH),
            transcendentals=0,
        ),
    )(info, where, regroup, xr, xl, zr)


def shards(samples, valid_counts, channel_mask, block_pairs):
    segs, channels, samples_len = samples.shape
    block_count = valid_counts.shape[0]
    planes = lax.axis_size("blk")
    peers = lax.axis_size("seg") * lax.axis_size("freq")
    pairs = block_pairs.shape[0]
    bins = samples_len // 2

    table, regroup = lax.optimization_barrier(
        (jnp.asarray(transform_table(bins, samples_len)), jnp.asarray(regroup_matrix()))
    )
    within = jnp.arange(WIDTH, dtype=jnp.int32)[None, :] < valid_counts[:, None]
    valid = (within & (channel_mask.reshape(block_count, WIDTH) == 1)).astype(jnp.int32)
    lines = jnp.pad(block_pairs.T, ((0, block_count - 2), (0, WIDTH - pairs)))
    own = jnp.concatenate([valid, lines], 0)
    others = [
        lax.ppermute(own, "blk", [(i, (i - shift) % planes) for i in range(planes)]) for shift in range(1, planes)
    ]
    me = lax.axis_index("blk").astype(jnp.int32).reshape(1, 1)
    place, where, info, branch = plan(me, own, others, block_count, pairs)
    place_row = place.reshape(1, channels)
    scale = 1.0 / math.sqrt(peers * segs)

    def with_sizes(r_count, l_count):
        def run(samples, table, regroup, place_row, where, info):
            own_r = spectra_chunk(samples, table, place_row, HB * WIDTH, whole_tiles(r_count) - r_count, r_count, peers, r_count < 320)
            xr = lax.all_to_all(own_r, ("seg", "freq"), split_axis=0, concat_axis=0, tiled=True)
            own_l = spectra_chunk(samples, table, place_row, channels, whole_tiles(r_count), l_count, peers, False)
            xr, own_l = lax.optimization_barrier((xr, own_l))
            zr = lax.ppermute(xr, "blk", [(i, i - 1) for i in range(1, planes)])
            info = after(info, zr)
            xl = lax.all_to_all(own_l, ("seg", "freq"), split_axis=0, concat_axis=0, tiled=True)
            return stacked_products(xr, xl, zr, info, where, regroup, pairs, scale)

        return run

    return lax.switch(
        branch[0, 0],
        [with_sizes(r, l) for r, l in SIZES],
        samples, table, regroup, place_row, where, info,
    )


def solution(mesh):
    placed = (P(("seg", "freq"), "blk", None), P("blk"), P("blk"), P("blk", None))
    return jax.shard_map(
        shards,
        mesh=mesh,
        in_specs=placed,
        out_specs=P("blk", ("seg", "freq"), None, None, None),
        check_vma=False,
    )
```

profile of v0, /device:TPU:2, one launch (start us, length us, event | category | flops | bytes accessed | tf_op | source)
XLA Modules:
  0.0 127.9 jit_solution(14694576602467646612)
XLA Ops:
  0.0 0.8 fusion.1
  0.8 0.7 pad_add_fusion.refs_1_
  1.4 0.0 copy-start.9
  1.4 1.5 %collective-permute-start.7 = (s32[16,128]{1,0:T(8,128)S(1)}, s32[16,128]{1,0:T(8,128)S(1)}, u32[]{:S(2)}, u32[]{:S(2)}) collective-permute-start(s32[16,128]{1,0:T(8,128)S(1)} %pad_add_fusion.refs_1_), channel_id=1, source_target_pairs={{0,1},{1,2},{2,3},{3,0},{4,5},{5,6},{6,7},{7,4},{8,9},{9,10},{10,1... | collective-permute-start | bytes 24584 | tf_op jit(solution)/shard_map/ppermute | solution.py:364
  2.9 1.0 collective-permute-start.6
  4.0 2.2 %collective-permute-start.5 = (s32[16,128]{1,0:T(8,128)S(1)}, s32[16,128]{1,0:T(8,128)S(1)}, u32[]{:S(2)}, u32[]{:S(2)}) collective-permute-start(s32[16,128]{1,0:T(8,128)S(1)} %pad_add_fusion.refs_1_), channel_id=1, source_target_pairs={{0,3},{1,0},{2,1},{3,2},{4,7},{5,4},{6,5},{7,6},{8,11},{9,8},{10,9... | collective-permute-start | bytes 24584 | tf_op jit(solution)/shard_map/ppermute | solution.py:364
  6.2 0.0 collective-permute-done.7.refs_4_
  6.2 0.0 copy-start.10
  6.2 1.9 %collective-permute-done.6.refs_3_ = s32[16,128]{1,0:T(8,128)S(1)} collective-permute-done((s32[16,128]{1,0:T(8,128)S(1)}, s32[16,128]{1,0:T(8,128)S(1)}, u32[]{:S(2)}, u32[]{:S(2)}) %collective-permute-start.6) | collective-permute-done | bytes 8224 | tf_op jit(solution)/shard_map/ppermute | solution.py:364
  8.1 0.0 copy-start.11
  8.1 0.0 collective-permute-done.5.refs_2_
  8.1 0.0 copy-start.12
  8.1 0.0 copy-done.9
  8.1 0.0 copy-done.10
  8.1 0.6 copy-done.11
  8.7 0.0 copy-done.12
  8.7 1.5 %shard_map.69 = (s32[8,128]{1,0:T(8,128)S(1)}, s32[8,128]{1,0:T(8,128)S(1)}, s32[8,128]{1,0:T(8,128)S(1)}, s32[1,1]{1,0:T(1,128)}) custom-call(s32[1,1]{1,0:T(1,128)} %bitcast.refs_0_, s32[16,128]{1,0:T(8,128)} %copy-done.9, s32[16,128]{1,0:T(8,128)} %copy-done.12, s32[16,128]{1,0:T(8,128)} %copy-done.11, s32[16,128]{1,0:T(8,128)} %copy-done.10), custom_call_target="tpu_custom_call" | custom-call | tf_op jit(solution)/shard_map/pallas_call | solution.py:125
  10.8 117.1 %conditional.1 = (bf16[4,32,2,128,128]{4,3,2,1,0:T(8,128)(2,1)}) conditional(s32[]{:T(128)} %bitcast.3, (s32[1,1024]{1,0:T(1,128)S(1)}, bf16[2,1024,2048]{2,1,0:T(8,128)(2,1)}, bf16[2048,2048]{1,0:T(8,128)(2,1)}, s32[8,128]{1,0:T(8,128)S(1)}, s32[8,128]{1,0:T(8,128)S(1)}, ...), branch_computations={%region_0.1_spmd, %region_1.2_spmd, %region_2.3_spmd, %region_3.4_... | conditional | flops 128991027200 | bytes 1166540928 | solution.py:384
  11.1 10.1 %branch_2_fun.4 = bf16[32,64,512]{2,1,0:T(8,128)(2,1)} custom-call(s32[1,1024]{1,0:T(1,128)S(1)} %get-tuple-element.88.refs_0_, bf16[2,1024,2048]{2,1,0:T(8,128)(2,1)} %get-tuple-element.89.refs_1_, bf16[2048,2048]{1,0:T(8,128)(2,1)} %get-tuple-element.90.refs_2_), custom_call_target="tpu_custom_call" | custom-call | flops 5368709120 | bytes 12582912 | tf_op jit(solution)/shard_map/cond/branch_2_fun/pallas_call | solution.py:215
  21.1 8.5 %all-to-all-start.4 = ((bf16[32,64,512]{2,1,0:T(8,128)(2,1)}), bf16[32,64,512]{2,1,0:T(8,128)(2,1)}, u32[]{:S(2)}, u32[]{:S(2)}) async-start(bf16[32,64,512]{2,1,0:T(8,128)(2,1)} %branch_2_fun.4), calls=%async_computation.4 | async-start | bytes 4194304 | tf_op jit(solution)/shard_map/cond/branch_2_fun/all_to_all | solution.py:374
  29.6 23.0 %branch_2_fun.5 = bf16[32,64,896]{2,1,0:T(8,128)(2,1)} custom-call(s32[1,1024]{1,0:T(1,128)S(1)} %get-tuple-element.88.refs_0_, bf16[2,1024,2048]{2,1,0:T(8,128)(2,1)} %get-tuple-element.89.refs_1_, bf16[2048,2048]{1,0:T(8,128)(2,1)} %get-tuple-element.90.refs_2_), custom_call_target="tpu_custom_call" | custom-call | flops 11274289152 | bytes 16777216 | tf_op jit(solution)/shard_map/cond/branch_2_fun/pallas_call | solution.py:215
  52.7 5.3 %all-to-all-done.4.refs_3_ = bf16[32,64,512]{2,1,0:T(8,128)(2,1)} async-done(((bf16[32,64,512]{2,1,0:T(8,128)(2,1)}), bf16[32,64,512]{2,1,0:T(8,128)(2,1)}, u32[]{:S(2)}, u32[]{:S(2)}) %all-to-all-start.4) | async-done | bytes 2097184 | tf_op jit(solution)/shard_map/cond/branch_2_fun/all_to_all | solution.py:374
  57.9 3.6 %collective-permute-start.2 = (bf16[32,64,512]{2,1,0:T(8,128)(2,1)}, bf16[32,64,512]{2,1,0:T(8,128)(2,1)S(1)}, u32[]{:S(2)}, u32[]{:S(2)}) collective-permute-start(bf16[32,64,512]{2,1,0:T(8,128)(2,1)} %all-to-all-done.4.refs_3_), channel_id=1, source_target_pairs={{1,0},{2,1},{3,2},{5,4},{6,5},{7,6},{9,8},{10,9},{11,10},{13,12},{... | collective-permute-start | bytes 6291464 | tf_op jit(solution)/shard_map/cond/branch_2_fun/ppermute | solution.py:377
  61.6 4.8 %all-to-all-start.5 = ((bf16[32,64,896]{2,1,0:T(8,128)(2,1)}), bf16[32,64,896]{2,1,0:T(8,128)(2,1)}, u32[]{:S(2)}, u32[]{:S(2)}) async-start(bf16[32,64,896]{2,1,0:T(8,128)(2,1)} %branch_2_fun.5), calls=%async_computation.5 | async-start | bytes 7340032 | tf_op jit(solution)/shard_map/cond/branch_2_fun/all_to_all | solution.py:379
  66.4 40.0 %collective-permute-done.2.other_ref.refs_5_ = bf16[32,64,512]{2,1,0:T(8,128)(2,1)S(1)} collective-permute-done((bf16[32,64,512]{2,1,0:T(8,128)(2,1)}, bf16[32,64,512]{2,1,0:T(8,128)(2,1)S(1)}, u32[]{:S(2)}, u32[]{:S(2)}) %collective-permute-start.2) | collective-permute-done | bytes 2097184 | tf_op jit(solution)/shard_map/cond/branch_2_fun/ppermute | solution.py:377
  106.5 0.0 copy-start.6
  106.5 1.3 %copy-done.6 = bf16[32,64,512]{2,1,0:T(8,128)(2,1)} copy-done((bf16[32,64,512]{2,1,0:T(8,128)(2,1)}, bf16[32,64,512]{2,1,0:T(8,128)(2,1)S(1)}, u32[]{:S(2)}) %copy-start.6) | copy-done | bytes 2097176 | tf_op jit(solution)/shard_map/cond
  107.8 0.0 copy-start.2
  107.8 4.0 %all-to-all-done.5.refs_4_ = bf16[32,64,896]{2,1,0:T(8,128)(2,1)} async-done(((bf16[32,64,896]{2,1,0:T(8,128)(2,1)}), bf16[32,64,896]{2,1,0:T(8,128)(2,1)}, u32[]{:S(2)}, u32[]{:S(2)}) %all-to-all-start.5) | async-done | bytes 3670048 | tf_op jit(solution)/shard_map/cond/branch_2_fun/all_to_all | solution.py:379
  111.8 0.0 copy-done.2
  111.8 16.1 %branch_2_fun.7 = bf16[4,32,2,128,128]{4,3,2,1,0:T(8,128)(2,1)} custom-call(s32[8,128]{1,0:T(8,128)S(1)} %branch_2_fun.6.refs_0_, s32[8,128]{1,0:T(8,128)S(1)} %get-tuple-element.92.refs_1_, bf16[256,256]{1,0:T(8,128)(2,1)S(1)} %copy-done.2, bf16[32,64,512]{2,1,0:T(8,128)(2,1)} %all-to-all-done.4.refs_3_, bf16[32,64,896]{2,1,0:T(8,128)(2,1)} %all-to-all-done.5.refs_4_, ...), custom_call_target="tpu_custom_call" | custom-call | flops 4160749568 | bytes 16252928 | tf_op jit(solution)/shard_map/cond/branch_2_fun/pallas_call | solution.py:325
  (1 shorter events, 0.0 us)
Async XLA Ops:
  1.4 6.7 %copy-start.9 = (s32[16,128]{1,0:T(8,128)}, s32[16,128]{1,0:T(8,128)S(1)}, u32[]{:S(2)}) copy-start(s32[16,128]{1,0:T(8,128)S(1)} %pad_add_fusion.refs_1_) | copy-start | bytes 24580
  1.4 4.8 %collective-permute-start.7 = (s32[16,128]{1,0:T(8,128)S(1)}, s32[16,128]{1,0:T(8,128)S(1)}, u32[]{:S(2)}, u32[]{:S(2)}) collective-permute-start(s32[16,128]{1,0:T(8,128)S(1)} %pad_add_fusion.refs_1_), channel_id=1, source_target_pairs={{0,1},{1,2},{2,3},{3,0},{4,5},{5,6},{6,7},{7,4},{8,9},{9,10},{10,1... | collective-permute-start | bytes 24584 | tf_op jit(solution)/shard_map/ppermute | solution.py:364
  2.9 5.2 %collective-permute-start.6 = (s32[16,128]{1,0:T(8,128)S(1)}, s32[16,128]{1,0:T(8,128)S(1)}, u32[]{:S(2)}, u32[]{:S(2)}) collective-permute-start(s32[16,128]{1,0:T(8,128)S(1)} %pad_add_fusion.refs_1_), channel_id=1, source_target_pairs={{0,2},{1,3},{2,0},{3,1},{4,6},{5,7},{6,4},{7,5},{8,10},{9,11},{10,... | collective-permute-start | bytes 24584 | tf_op jit(solution)/shard_map/ppermute | solution.py:364
  4.0 4.1 %collective-permute-start.5 = (s32[16,128]{1,0:T(8,128)S(1)}, s32[16,128]{1,0:T(8,128)S(1)}, u32[]{:S(2)}, u32[]{:S(2)}) collective-permute-start(s32[16,128]{1,0:T(8,128)S(1)} %pad_add_fusion.refs_1_), channel_id=1, source_target_pairs={{0,3},{1,0},{2,1},{3,2},{4,7},{5,4},{6,5},{7,6},{8,11},{9,8},{10,9... | collective-permute-start | bytes 24584 | tf_op jit(solution)/shard_map/ppermute | solution.py:364
  6.2 1.9 %copy-start.10 = (s32[16,128]{1,0:T(8,128)}, s32[16,128]{1,0:T(8,128)S(1)}, u32[]{:S(2)}) copy-start(s32[16,128]{1,0:T(8,128)S(1)} %collective-permute-done.7.refs_4_) | copy-start | bytes 24580
  8.1 0.6 copy-start.11
  8.1 0.6 copy-start.12
  21.1 36.8 %all-to-all-start.4 = ((bf16[32,64,512]{2,1,0:T(8,128)(2,1)}), bf16[32,64,512]{2,1,0:T(8,128)(2,1)}, u32[]{:S(2)}, u32[]{:S(2)}) async-start(bf16[32,64,512]{2,1,0:T(8,128)(2,1)} %branch_2_fun.4), calls=%async_computation.4 | async-start | bytes 4194304 | tf_op jit(solution)/shard_map/cond/branch_2_fun/all_to_all | solution.py:374
  57.9 48.5 %collective-permute-start.2 = (bf16[32,64,512]{2,1,0:T(8,128)(2,1)}, bf16[32,64,512]{2,1,0:T(8,128)(2,1)S(1)}, u32[]{:S(2)}, u32[]{:S(2)}) collective-permute-start(bf16[32,64,512]{2,1,0:T(8,128)(2,1)} %all-to-all-done.4.refs_3_), channel_id=1, source_target_pairs={{1,0},{2,1},{3,2},{5,4},{6,5},{7,6},{9,8},{10,9},{11,10},{13,12},{... | collective-permute-start | bytes 6291464 | tf_op jit(solution)/shard_map/cond/branch_2_fun/ppermute | solution.py:377
  61.6 50.2 %all-to-all-start.5 = ((bf16[32,64,896]{2,1,0:T(8,128)(2,1)}), bf16[32,64,896]{2,1,0:T(8,128)(2,1)}, u32[]{:S(2)}, u32[]{:S(2)}) async-start(bf16[32,64,896]{2,1,0:T(8,128)(2,1)} %branch_2_fun.5), calls=%async_computation.5 | async-start | bytes 7340032 | tf_op jit(solution)/shard_map/cond/branch_2_fun/all_to_all | solution.py:379
  106.5 1.3 %copy-start.6 = (bf16[32,64,512]{2,1,0:T(8,128)(2,1)}, bf16[32,64,512]{2,1,0:T(8,128)(2,1)S(1)}, u32[]{:S(2)}) copy-start(bf16[32,64,512]{2,1,0:T(8,128)(2,1)S(1)} %collective-permute-done.2.other_ref.refs_5_) | copy-start | bytes 6291460 | tf_op jit(solution)/shard_map/cond
  107.8 4.0 %copy-start.2 = (bf16[256,256]{1,0:T(8,128)(2,1)S(1)}, bf16[256,256]{1,0:T(8,128)(2,1)}, u32[]{:S(2)}) copy-start(bf16[256,256]{1,0:T(8,128)(2,1)} %get-tuple-element.93.refs_2_) | copy-start | bytes 393220 | tf_op jit(solution)/shard_map/cond
where the time goes:
time: 128 us
  waiting for transfers between devices  51.2 us (40%)
  Pallas kernels  50.7 us (40%)
  starting transfers between devices  21.7 us (17%)
  local copies, waits for them, and re-layouts  1.93 us (2%)
  other arithmetic  1.44 us (1%)
    ppermute x1, waiting for transfers between devices, run(): zr = lax.ppermute(xr, 'blk', [(i, i - 1) for i in range(1, planes)])  40 us
    pallas_call x2, Pallas kernels, spectra_chunk(): pl.pallas_call(body, in_specs=[vmem, hbm, hbm], out_specs=hbm, out_shape=...  33.1 us
    pallas_call x1, Pallas kernels, stacked_products(): pl.pallas_call(body, grid=(bins // group,), in_specs=[pl.BlockSpec(memory...  16.1 us
    all_to_all x1, starting transfers between devices, run(): lax.all_to_all(own_r, ('seg', 'freq'), split_axis=0, concat_axis=0, tiled...  8.47 us
    all_to_all x1, waiting for transfers between devices, run(): lax.all_to_all(own_r, ('seg', 'freq'), split_axis=0, concat_axis=0, tiled...  5.25 us
    all_to_all x1, starting transfers between devices, run(): lax.all_to_all(own_l, ('seg', 'freq'), split_axis=0, concat_axis=0, tiled...  4.85 us
    ppermute x3, starting transfers between devices, shards(): lax.ppermute(own, 'blk', [(i, (i - shift) % planes) for i in range(planes)])  4.76 us
    all_to_all x1, waiting for transfers between devices, run(): lax.all_to_all(own_l, ('seg', 'freq'), split_axis=0, concat_axis=0, tiled...  4.04 us
  transfers between devices with their start and end apart: 6, of which 4 were waited for; matrix products, arithmetic and copies ran while one was open for 0% of the time, Pallas kernels for 18%

commit v1 on v0

--- a/solution.py
+++ b/solution.py
@@ -207,7 +207,7 @@
     segs, _, samples_len = samples.shape
     rows_total = table.shape[0]
     lanes = segs * count
-    pieces, tile, across = (4, 1024, lanes) if urgent else (4, 256, 256)
+    pieces, tile, across = (4, 1024, lanes) if urgent else (4, 512 if count <= 320 and channels > HB * WIDTH else 256, 256)
     wide = (lanes + across - 1) // across * across
     body = lambda *refs: spectra_kernel(base, count, tile, across, *refs)
     hbm = pl.BlockSpec(memory_space=pl.ANY)

time: 128 us -> 128 us (level)
  no operation moved by 1% of the time
where the time goes in v1:
time: 128 us
  waiting for transfers between devices  51.2 us (40%)
  Pallas kernels  50.7 us (40%)
  starting transfers between devices  21.7 us (17%)
  local copies, waits for them, and re-layouts  1.93 us (2%)
  other arithmetic  1.44 us (1%)
    ppermute x1, waiting for transfers between devices, run(): zr = lax.ppermute(xr, 'blk', [(i, i - 1) for i in range(1, planes)])  40 us
    pallas_call x2, Pallas kernels, spectra_chunk(): pl.pallas_call(body, in_specs=[vmem, hbm, hbm], out_specs=hbm, out_shape=...  33.1 us
    pallas_call x1, Pallas kernels, stacked_products(): pl.pallas_call(body, grid=(bins // group,), in_specs=[pl.BlockSpec(memory...  16.1 us
    all_to_all x1, starting transfers between devices, run(): lax.all_to_all(own_r, ('seg', 'freq'), split_axis=0, concat_axis=0, tiled...  8.47 us
    all_to_all x1, waiting for transfers between devices, run(): lax.all_to_all(own_r, ('seg', 'freq'), split_axis=0, concat_axis=0, tiled...  5.25 us
    all_to_all x1, starting transfers between devices, run(): lax.all_to_all(own_l, ('seg', 'freq'), split_axis=0, concat_axis=0, tiled...  4.85 us
    ppermute x3, starting transfers between devices, shards(): lax.ppermute(own, 'blk', [(i, (i - shift) % planes) for i in range(planes)])  4.76 us
    all_to_all x1, waiting for transfers between devices, run(): lax.all_to_all(own_l, ('seg', 'freq'), split_axis=0, concat_axis=0, tiled...  4.04 us
  transfers between devices with their start and end apart: 6, of which 4 were waited for; matrix products, arithmetic and copies ran while one was open for 0% of the time, Pallas kernels for 18%

profile of v1, /device:TPU:2, one launch (start us, length us, event | category | flops | bytes accessed | tf_op | source)
XLA Modules:
  0.0 128.0 jit_solution(18180968830966424214)
XLA Ops:
  0.0 0.8 fusion.1
  0.8 0.7 pad_add_fusion.refs_1_
  1.4 0.0 copy-start.9
  1.4 1.5 %collective-permute-start.7 = (s32[16,128]{1,0:T(8,128)S(1)}, s32[16,128]{1,0:T(8,128)S(1)}, u32[]{:S(2)}, u32[]{:S(2)}) collective-permute-start(s32[16,128]{1,0:T(8,128)S(1)} %pad_add_fusion.refs_1_), channel_id=1, source_target_pairs={{0,1},{1,2},{2,3},{3,0},{4,5},{5,6},{6,7},{7,4},{8,9},{9,10},{10,1... | collective-permute-start | bytes 24584 | tf_op jit(solution)/shard_map/ppermute | solution.py:364
  2.9 1.0 collective-permute-start.6
  4.0 2.2 %collective-permute-start.5 = (s32[16,128]{1,0:T(8,128)S(1)}, s32[16,128]{1,0:T(8,128)S(1)}, u32[]{:S(2)}, u32[]{:S(2)}) collective-permute-start(s32[16,128]{1,0:T(8,128)S(1)} %pad_add_fusion.refs_1_), channel_id=1, source_target_pairs={{0,3},{1,0},{2,1},{3,2},{4,7},{5,4},{6,5},{7,6},{8,11},{9,8},{10,9... | collective-permute-start | bytes 24584 | tf_op jit(solution)/shard_map/ppermute | solution.py:364
  6.2 0.0 collective-permute-done.7.refs_4_
  6.2 0.0 copy-start.10
  6.2 1.9 %collective-permute-done.6.refs_3_ = s32[16,128]{1,0:T(8,128)S(1)} collective-permute-done((s32[16,128]{1,0:T(8,128)S(1)}, s32[16,128]{1,0:T(8,128)S(1)}, u32[]{:S(2)}, u32[]{:S(2)}) %collective-permute-start.6) | collective-permute-done | bytes 8224 | tf_op jit(solution)/shard_map/ppermute | solution.py:364
  8.1 0.0 copy-start.11
  8.1 0.0 collective-permute-done.5.refs_2_
  8.1 0.0 copy-start.12
  8.1 0.0 copy-done.9
  8.1 0.0 copy-done.10
  8.1 0.6 copy-done.11
  8.7 0.0 copy-done.12
  8.7 1.5 %shard_map.69 = (s32[8,128]{1,0:T(8,128)S(1)}, s32[8,128]{1,0:T(8,128)S(1)}, s32[8,128]{1,0:T(8,128)S(1)}, s32[1,1]{1,0:T(1,128)}) custom-call(s32[1,1]{1,0:T(1,128)} %bitcast.refs_0_, s32[16,128]{1,0:T(8,128)} %copy-done.9, s32[16,128]{1,0:T(8,128)} %copy-done.12, s32[16,128]{1,0:T(8,128)} %copy-done.11, s32[16,128]{1,0:T(8,128)} %copy-done.10), custom_call_target="tpu_custom_call" | custom-call | tf_op jit(solution)/shard_map/pallas_call | solution.py:125
  10.8 117.1 %conditional.1 = (bf16[4,32,2,128,128]{4,3,2,1,0:T(8,128)(2,1)}) conditional(s32[]{:T(128)} %bitcast.3, (s32[1,1024]{1,0:T(1,128)S(1)}, bf16[2,1024,2048]{2,1,0:T(8,128)(2,1)}, bf16[2048,2048]{1,0:T(8,128)(2,1)}, s32[8,128]{1,0:T(8,128)S(1)}, s32[8,128]{1,0:T(8,128)S(1)}, ...), branch_computations={%region_0.1_spmd, %region_1.2_spmd, %region_2.3_spmd, %region_3.4_... | conditional | flops 128991027200 | bytes 1166540928 | solution.py:384
  11.1 10.1 %branch_2_fun.4 = bf16[32,64,512]{2,1,0:T(8,128)(2,1)} custom-call(s32[1,1024]{1,0:T(1,128)S(1)} %get-tuple-element.88.refs_0_, bf16[2,1024,2048]{2,1,0:T(8,128)(2,1)} %get-tuple-element.89.refs_1_, bf16[2048,2048]{1,0:T(8,128)(2,1)} %get-tuple-element.90.refs_2_), custom_call_target="tpu_custom_call" | custom-call | flops 5368709120 | bytes 12582912 | tf_op jit(solution)/shard_map/cond/branch_2_fun/pallas_call | solution.py:215
  21.1 8.5 %all-to-all-start.4 = ((bf16[32,64,512]{2,1,0:T(8,128)(2,1)}), bf16[32,64,512]{2,1,0:T(8,128)(2,1)}, u32[]{:S(2)}, u32[]{:S(2)}) async-start(bf16[32,64,512]{2,1,0:T(8,128)(2,1)} %branch_2_fun.4), calls=%async_computation.4 | async-start | bytes 4194304 | tf_op jit(solution)/shard_map/cond/branch_2_fun/all_to_all | solution.py:374
  29.6 23.0 %branch_2_fun.5 = bf16[32,64,896]{2,1,0:T(8,128)(2,1)} custom-call(s32[1,1024]{1,0:T(1,128)S(1)} %get-tuple-element.88.refs_0_, bf16[2,1024,2048]{2,1,0:T(8,128)(2,1)} %get-tuple-element.89.refs_1_, bf16[2048,2048]{1,0:T(8,128)(2,1)} %get-tuple-element.90.refs_2_), custom_call_target="tpu_custom_call" | custom-call | flops 11274289152 | bytes 16777216 | tf_op jit(solution)/shard_map/cond/branch_2_fun/pallas_call | solution.py:215
  52.7 5.3 %all-to-all-done.4.refs_3_ = bf16[32,64,512]{2,1,0:T(8,128)(2,1)} async-done(((bf16[32,64,512]{2,1,0:T(8,128)(2,1)}), bf16[32,64,512]{2,1,0:T(8,128)(2,1)}, u32[]{:S(2)}, u32[]{:S(2)}) %all-to-all-start.4) | async-done | bytes 2097184 | tf_op jit(solution)/shard_map/cond/branch_2_fun/all_to_all | solution.py:374
  57.9 3.6 %collective-permute-start.2 = (bf16[32,64,512]{2,1,0:T(8,128)(2,1)}, bf16[32,64,512]{2,1,0:T(8,128)(2,1)S(1)}, u32[]{:S(2)}, u32[]{:S(2)}) collective-permute-start(bf16[32,64,512]{2,1,0:T(8,128)(2,1)} %all-to-all-done.4.refs_3_), channel_id=1, source_target_pairs={{1,0},{2,1},{3,2},{5,4},{6,5},{7,6},{9,8},{10,9},{11,10},{13,12},{... | collective-permute-start | bytes 6291464 | tf_op jit(solution)/shard_map/cond/branch_2_fun/ppermute | solution.py:377
  61.6 4.8 %all-to-all-start.5 = ((bf16[32,64,896]{2,1,0:T(8,128)(2,1)}), bf16[32,64,896]{2,1,0:T(8,128)(2,1)}, u32[]{:S(2)}, u32[]{:S(2)}) async-start(bf16[32,64,896]{2,1,0:T(8,128)(2,1)} %branch_2_fun.5), calls=%async_computation.5 | async-start | bytes 7340032 | tf_op jit(solution)/shard_map/cond/branch_2_fun/all_to_all | solution.py:379
  66.4 40.0 %collective-permute-done.2.other_ref.refs_5_ = bf16[32,64,512]{2,1,0:T(8,128)(2,1)S(1)} collective-permute-done((bf16[32,64,512]{2,1,0:T(8,128)(2,1)}, bf16[32,64,512]{2,1,0:T(8,128)(2,1)S(1)}, u32[]{:S(2)}, u32[]{:S(2)}) %collective-permute-start.2) | collective-permute-done | bytes 2097184 | tf_op jit(solution)/shard_map/cond/branch_2_fun/ppermute | solution.py:377
  106.5 0.0 copy-start.6
  106.5 1.3 %copy-done.6 = bf16[32,64,512]{2,1,0:T(8,128)(2,1)} copy-done((bf16[32,64,512]{2,1,0:T(8,128)(2,1)}, bf16[32,64,512]{2,1,0:T(8,128)(2,1)S(1)}, u32[]{:S(2)}) %copy-start.6) | copy-done | bytes 2097176 | tf_op jit(solution)/shard_map/cond
  107.8 0.0 copy-start.2
  107.8 4.0 %all-to-all-done.5.refs_4_ = bf16[32,64,896]{2,1,0:T(8,128)(2,1)} async-done(((bf16[32,64,896]{2,1,0:T(8,128)(2,1)}), bf16[32,64,896]{2,1,0:T(8,128)(2,1)}, u32[]{:S(2)}, u32[]{:S(2)}) %all-to-all-start.5) | async-done | bytes 3670048 | tf_op jit(solution)/shard_map/cond/branch_2_fun/all_to_all | solution.py:379
  111.8 0.0 copy-done.2
  111.8 16.1 %branch_2_fun.7 = bf16[4,32,2,128,128]{4,3,2,1,0:T(8,128)(2,1)} custom-call(s32[8,128]{1,0:T(8,128)S(1)} %branch_2_fun.6.refs_0_, s32[8,128]{1,0:T(8,128)S(1)} %get-tuple-element.92.refs_1_, bf16[256,256]{1,0:T(8,128)(2,1)S(1)} %copy-done.2, bf16[32,64,512]{2,1,0:T(8,128)(2,1)} %all-to-all-done.4.refs_3_, bf16[32,64,896]{2,1,0:T(8,128)(2,1)} %all-to-all-done.5.refs_4_, ...), custom_call_target="tpu_custom_call" | custom-call | flops 4160749568 | bytes 16252928 | tf_op jit(solution)/shard_map/cond/branch_2_fun/pallas_call | solution.py:325
  (1 shorter events, 0.0 us)
Async XLA Ops:
  1.4 6.7 %copy-start.9 = (s32[16,128]{1,0:T(8,128)}, s32[16,128]{1,0:T(8,128)S(1)}, u32[]{:S(2)}) copy-start(s32[16,128]{1,0:T(8,128)S(1)} %pad_add_fusion.refs_1_) | copy-start | bytes 24580
  1.4 4.8 %collective-permute-start.7 = (s32[16,128]{1,0:T(8,128)S(1)}, s32[16,128]{1,0:T(8,128)S(1)}, u32[]{:S(2)}, u32[]{:S(2)}) collective-permute-start(s32[16,128]{1,0:T(8,128)S(1)} %pad_add_fusion.refs_1_), channel_id=1, source_target_pairs={{0,1},{1,2},{2,3},{3,0},{4,5},{5,6},{6,7},{7,4},{8,9},{9,10},{10,1... | collective-permute-start | bytes 24584 | tf_op jit(solution)/shard_map/ppermute | solution.py:364
  2.9 5.2 %collective-permute-start.6 = (s32[16,128]{1,0:T(8,128)S(1)}, s32[16,128]{1,0:T(8,128)S(1)}, u32[]{:S(2)}, u32[]{:S(2)}) collective-permute-start(s32[16,128]{1,0:T(8,128)S(1)} %pad_add_fusion.refs_1_), channel_id=1, source_target_pairs={{0,2},{1,3},{2,0},{3,1},{4,6},{5,7},{6,4},{7,5},{8,10},{9,11},{10,... | collective-permute-start | bytes 24584 | tf_op jit(solution)/shard_map/ppermute | solution.py:364
  4.0 4.1 %collective-permute-start.5 = (s32[16,128]{1,0:T(8,128)S(1)}, s32[16,128]{1,0:T(8,128)S(1)}, u32[]{:S(2)}, u32[]{:S(2)}) collective-permute-start(s32[16,128]{1,0:T(8,128)S(1)} %pad_add_fusion.refs_1_), channel_id=1, source_target_pairs={{0,3},{1,0},{2,1},{3,2},{4,7},{5,4},{6,5},{7,6},{8,11},{9,8},{10,9... | collective-permute-start | bytes 24584 | tf_op jit(solution)/shard_map/ppermute | solution.py:364
  6.2 1.9 %copy-start.10 = (s32[16,128]{1,0:T(8,128)}, s32[16,128]{1,0:T(8,128)S(1)}, u32[]{:S(2)}) copy-start(s32[16,128]{1,0:T(8,128)S(1)} %collective-permute-done.7.refs_4_) | copy-start | bytes 24580
  8.1 0.6 copy-start.11
  8.1 0.6 copy-start.12
  21.1 36.8 %all-to-all-start.4 = ((bf16[32,64,512]{2,1,0:T(8,128)(2,1)}), bf16[32,64,512]{2,1,0:T(8,128)(2,1)}, u32[]{:S(2)}, u32[]{:S(2)}) async-start(bf16[32,64,512]{2,1,0:T(8,128)(2,1)} %branch_2_fun.4), calls=%async_computation.4 | async-start | bytes 4194304 | tf_op jit(solution)/shard_map/cond/branch_2_fun/all_to_all | solution.py:374
  57.9 48.5 %collective-permute-start.2 = (bf16[32,64,512]{2,1,0:T(8,128)(2,1)}, bf16[32,64,512]{2,1,0:T(8,128)(2,1)S(1)}, u32[]{:S(2)}, u32[]{:S(2)}) collective-permute-start(bf16[32,64,512]{2,1,0:T(8,128)(2,1)} %all-to-all-done.4.refs_3_), channel_id=1, source_target_pairs={{1,0},{2,1},{3,2},{5,4},{6,5},{7,6},{9,8},{10,9},{11,10},{13,12},{... | collective-permute-start | bytes 6291464 | tf_op jit(solution)/shard_map/cond/branch_2_fun/ppermute | solution.py:377
  61.6 50.2 %all-to-all-start.5 = ((bf16[32,64,896]{2,1,0:T(8,128)(2,1)}), bf16[32,64,896]{2,1,0:T(8,128)(2,1)}, u32[]{:S(2)}, u32[]{:S(2)}) async-start(bf16[32,64,896]{2,1,0:T(8,128)(2,1)} %branch_2_fun.5), calls=%async_computation.5 | async-start | bytes 7340032 | tf_op jit(solution)/shard_map/cond/branch_2_fun/all_to_all | solution.py:379
  106.5 1.3 %copy-start.6 = (bf16[32,64,512]{2,1,0:T(8,128)(2,1)}, bf16[32,64,512]{2,1,0:T(8,128)(2,1)S(1)}, u32[]{:S(2)}) copy-start(bf16[32,64,512]{2,1,0:T(8,128)(2,1)S(1)} %collective-permute-done.2.other_ref.refs_5_) | copy-start | bytes 6291460 | tf_op jit(solution)/shard_map/cond
  107.8 4.0 %copy-start.2 = (bf16[256,256]{1,0:T(8,128)(2,1)S(1)}, bf16[256,256]{1,0:T(8,128)(2,1)}, u32[]{:S(2)}) copy-start(bf16[256,256]{1,0:T(8,128)(2,1)} %get-tuple-element.93.refs_2_) | copy-start | bytes 393220 | tf_op jit(solution)/shard_map/cond
